TPU v7x, 32 devices: a whole 2x2x4 slice. The times are simulated.
32 devices in a mesh: cell: 8 (over z, y), stn: 4 (over x, core).
Axes of the slice: x: 2, y: 2, z: 4, core: 2. Of those that a mesh axis runs over, the one named last changes fastest.
Arguments:
- cell_points: float32 [3, 8192], P(None, 'cell'), may hold values from 0 to 1
- magnetization: float32 [3, 8192], P(None, 'cell'), may hold values from -6 to 6
- cell_level: int32 [8192], P('cell'), may hold values from 0 to 2
- suscept: float32 [8192], P('cell'), may hold values from 0.2 to 2
- inducing: float32 [3], replicated, may hold values from -4 to 4
- stations: float32 [3, 4096], P(None, 'stn'), may hold values from 0 to 2, as said below
Outputs:
- updated: float32 [3, 8192], P(None, ('cell', 'stn'))
- predictions: float32 [4096], P(('stn', 'cell'))
Inputs may be any that keep to these rules, and one draw needn't show every extreme that they name: `stations`: the first two coordinates lie in the unit square; the third is 1 plus 0.5 to 2 times 8192 ** (-1/3).
All inputs are finite; a program needn't handle non-finite values.
Results may differ from a plain program's by a relative error of at most 0.0003.
Values sent between devices are 32-bit elements; how exact they have to be, the bound alone decides.
A program may use at most 64 MiB of HBM per device.

v0:
```python
import math
import jax
import jax.numpy as jnp
from jax import lax
from jax.sharding import PartitionSpec as P

INV_FOUR_PI = 0.25 / math.pi


def block_width(targets, sources):
    ceiling = max(256, (1 << 20) // targets)
    ceiling = 1 << ceiling.bit_length() - 1
    return math.gcd(sources, ceiling)


def pair_field(points, source_piece):
    delta_x = points[0][:, None] - source_piece[0][None, :]
    delta_y = points[1][:, None] - source_piece[1][None, :]
    delta_z = points[2][:, None] - source_piece[2][None, :]
    soften = source_piece[6][None, :]
    radius_sq = delta_x * delta_x + delta_y * delta_y + delta_z * delta_z + soften * soften
    inverse = lax.rsqrt(radius_sq)
    inverse_sq = inverse * inverse
    weight = INV_FOUR_PI * soften * soften * soften * inverse_sq * inverse
    projection = (
        3.0
        * (
            delta_x * source_piece[3][None, :]
            + delta_y * source_piece[4][None, :]
            + delta_z * source_piece[5][None, :]
        )
        * inverse_sq
    )
    field_x = jnp.sum(weight * (projection * delta_x - source_piece[3][None, :]), axis=1)
    field_y = jnp.sum(weight * (projection * delta_y - source_piece[4][None, :]), axis=1)
    field_z = jnp.sum(weight * (projection * delta_z - source_piece[5][None, :]), axis=1)
    return jnp.stack([field_x, field_y, field_z], 0)


def source_field(points, sources):
    number = sources.shape[1]
    blockw = block_width(points.shape[1], number)
    groups = sources.reshape(7, number // blockw, blockw).transpose(1, 0, 2)

    def advance(summed, source_piece):
        return (summed + pair_field(points, source_piece), None)

    result, unused = lax.scan(advance, jnp.zeros((3, points.shape[1]), jnp.float32), groups)
    return result


def shards(cell_points, magnetization, cell_level, suscept, inducing, stations):
    cycle_size = lax.axis_size("cell")
    section = lax.axis_size("stn")
    block_cells = cell_points.shape[1]
    spacing = float(block_cells * cycle_size * section // section) ** (-1.0 / 3.0)
    size_h = spacing * jnp.power(0.5, cell_level.astype(jnp.float32))
    packed = jnp.concatenate([cell_points, magnetization, size_h[None, :]], 0)
    owned = block_cells // section
    offset = lax.axis_index("stn") * owned
    targets = lax.dynamic_slice_in_dim(cell_points, offset, owned, 1)
    demag = source_field(targets, lax.all_gather(packed, "cell", axis=1, tiled=True))
    own_suscept = lax.dynamic_slice_in_dim(suscept, offset, owned, 0)
    updated = own_suscept[None, :] * (inducing[:, None] + demag)
    block_mag = lax.all_gather(updated, "stn", axis=1, tiled=True)
    moved = jnp.concatenate([cell_points, block_mag, size_h[None, :]], 0)
    field = source_field(stations, moved)
    predictions = lax.psum_scatter(
        jnp.sum(inducing[:, None] * field, axis=0), "cell", scatter_dimension=0, tiled=True
    )
    return (updated, predictions)


def solution(mesh):
    placed = (P(None, "cell"), P(None, "cell"), P("cell"), P("cell"), P(), P(None, "stn"))
    return jax.shard_map(
        shards,
        mesh=mesh,
        in_specs=placed,
        out_specs=(P(None, ("cell", "stn")), P(("stn", "cell"))),
        check_vma=False,
    )
```

profile of v0, /device:TPU:0, one launch (start us, length us, event | category | flops | bytes accessed | tf_op | source)
XLA Modules:
  0.0 82.9 jit_solution(14544340827631167878)
XLA Ops:
  0.6 0.7 constant_dynamic-slice_fusion.7
  1.3 0.7 multiply_multiply_fusion.3
  2.0 0.8 pad_maximum_fusion
  2.8 32.5 %all_gather.6 = f32[7,8192]{1,0:T(8,128)S(1)} all-gather(f32[7,1024]{1,0:T(8,128)S(1)} %pad_maximum_fusion), channel_id=1, replica_groups=mesh['cell'=8,'stn'=4] {'cell'}, dimensions={1}, use_global_device_ids=true | all-gather | bytes 258048 | tf_op jit(solution)/shard_map/all_gather | solution.py:62
  35.3 0.0 copy-start.3
  35.3 0.0 copy-start.2
  35.3 0.0 copy-start
  35.3 11.8 %while.3 = (s32[]{:T(128)}, f32[3,256]{1,0:T(4,128)S(1)}, f32[2,7,4096]{2,1,0:T(8,128)S(1)}, f32[3,256]{1,0:T(4,128)S(1)}, s32[]{:T(128)}, /*index=5*/s32[]{:T(128)}, s32[]{}, s32[]{}, s32[]{}, s32[]{}, /*index=10*/s32[]{}, s32[]{}) while((s32[]{:T(128)}, f32[3,256]{1,0:T(4,128)S(1)}, f32[2,7,4096]{2,1,0:T(8,128)S(1)}, ...), condition=%wide.region_4.5_spmd.clone, body=%wide.region_0.4_spmd.clone.sunk | while | flops 32524552 | bytes 431331 | solution.py:48
  35.3 0.1 constant_dynamic-slice_fusion.9
  35.5 5.7 %fusion.44 = (f32[256]{0:T(256)S(1)}, f32[256]{0:T(256)S(1)}, f32[256]{0:T(256)S(1)}) fusion(f32[4096]{0:T(1024)S(1)} %bitcast.60, f32[4096]{0:T(1024)S(1)} %bitcast.62, f32[256]{0:T(256)S(1)} %bitcast.69, f32[4096]{0:T(1024)S(1)} %get-tuple-element.134, f32[4096]{0:T(1024)S(1)} %bitcast.63, f32[4096]{0:T(1024)S(1)} %bitcast.61, f32[256]{0:T(256)S(1)} %bitcast.68, ...), kind=kLoop, calls=%fused_computation.19.clone.1 | loop fusion | flops 32505088 | bytes 137216 | tf_op jit(solution)/shard_map/while/body/eval_jaxpr/reduce_sum | solution.py:34
  41.2 0.1 constant_dynamic-slice_fusion.9
  41.4 5.7 %fusion.44 = (f32[256]{0:T(256)S(1)}, f32[256]{0:T(256)S(1)}, f32[256]{0:T(256)S(1)}) fusion(f32[4096]{0:T(1024)S(1)} %bitcast.60, f32[4096]{0:T(1024)S(1)} %bitcast.62, f32[256]{0:T(256)S(1)} %bitcast.69, f32[4096]{0:T(1024)S(1)} %get-tuple-element.134, f32[4096]{0:T(1024)S(1)} %bitcast.63, f32[4096]{0:T(1024)S(1)} %bitcast.61, f32[256]{0:T(256)S(1)} %bitcast.68, ...), kind=kLoop, calls=%fused_computation.19.clone.1 | loop fusion | flops 32505088 | bytes 137216 | tf_op jit(solution)/shard_map/while/body/eval_jaxpr/reduce_sum | solution.py:34
  47.2 0.8 dynamic_slice.13
  47.9 0.0 copy-done.3
  47.9 0.1 add_multiply_fusion
  48.0 0.0 copy-start.1
  48.0 5.2 %all_gather.7 = f32[3,1024]{1,0:T(4,128)S(1)} all-gather(f32[3,256]{1,0:T(4,128)S(1)} %add_multiply_fusion), channel_id=1, replica_groups=mesh['cell'=8,'stn'=4] {'stn'}, dimensions={1}, use_global_device_ids=true | all-gather | bytes 15360 | tf_op jit(solution)/shard_map/all_gather | solution.py:65
  53.2 0.0 copy-done.2
  53.2 0.0 copy-done
  53.2 0.0 copy-start.4
  53.3 6.2 %fusion.27 = (f32[1024]{0:T(1024)S(1)}, f32[1024]{0:T(1024)S(1)}, f32[1024]{0:T(1024)S(1)}) fusion(f32[1024]{0:T(1024)S(1)} %bitcast.73, f32[1024]{0:T(1024)S(1)} %bitcast.78, f32[1024]{0:T(1024)S(1)} %bitcast.75, f32[1024]{0:T(1024)S(1)} %get-tuple-element.88, f32[1024]{0:T(1024)S(1)} %bitcast.72, f32[1024]{0:T(1024)S(1)} %bitcast.79, ...), kind=kLoop, calls=%fused_computation.55 | loop fusion | flops 32502784 | bytes 57344 | tf_op jit(solution)/shard_map/while/body/eval_jaxpr/reduce_sum | solution.py:34
  59.5 0.0 copy-done.1
  59.5 0.1 fusion.34
  59.6 21.4 %all-reduce = f32[1024]{0:T(1024)S(1)} all-reduce(f32[1024]{0:T(1024)S(1)} %fusion.34), channel_id=2, replica_groups=mesh['cell'=8,'stn'=4] {'cell'}, use_global_device_ids=true, to_apply=%region_9.10.clone | all-reduce | flops 1024 | bytes 8192
  81.0 0.0 copy-done.4
  81.0 0.6 dynamic-slice.1
  82.3 0.6 dynamic-slice.2
  (10 shorter events, 0.1 us)
Async XLA Ops:
  35.3 12.6 %copy-start.3 = (f32[3]{0:T(128)S(1)}, f32[3]{0:T(128)}, u32[]{:S(2)}) copy-start(f32[3]{0:T(128)} %param.12) | copy-start | bytes 40
  35.3 17.9 %copy-start.2 = (f32[3,1024]{1,0:T(4,128)S(1)}, f32[3,1024]{1,0:T(4,128)}, u32[]{:S(2)}) copy-start(f32[3,1024]{1,0:T(4,128)} %param.13) | copy-start | bytes 36868
  35.3 17.9 %copy-start = (f32[3,1024]{1,0:T(4,128)S(1)}, f32[3,1024]{1,0:T(4,128)}, u32[]{:S(2)}) copy-start(f32[3,1024]{1,0:T(4,128)} %param.8) | copy-start | bytes 36868
  48.0 11.5 %copy-start.1 = (f32[3,256]{1,0:T(4,128)}, f32[3,256]{1,0:T(4,128)S(1)}, u32[]{:S(2)}) copy-start(f32[3,256]{1,0:T(4,128)S(1)} %add_multiply_fusion) | copy-start | bytes 9220
  53.2 27.8 %copy-start.4 = (u32[32]{0:T(128)S(1)}, u32[32]{0:T(128)}, u32[]{:S(2)}) copy-start(u32[32]{0:T(128)} %constant.48) | copy-start | bytes 388
where the time goes:
time: 83.3 us; the launch traced here: 82.9 us
  blocking collectives  59.1 us (71%)
  other arithmetic  19.4 us (23%)
  local copies, waits for them, and re-layouts  2.93 us (4%)
  between operations  1.37 us (2%)
    all_gather x1, blocking collectives, shards(): lax.all_gather(packed, 'cell', axis=1, tiled=True)  32.5 us
    unnamed x1, blocking collectives  21.4 us
    reduce_sum x3, other arithmetic, pair_field(): jnp.sum(weight * (projection * delta_x - source_piece[3][None, :]), axis=1)  17.7 us
    all_gather x1, blocking collectives, shards(): block_mag = lax.all_gather(updated, 'stn', axis=1, tiled=True)  5.17 us

commit v1 on v0

--- a/solution.py
+++ b/solution.py
@@ -62,7 +62,12 @@
     demag = source_field(targets, lax.all_gather(packed, "cell", axis=1, tiled=True))
     own_suscept = lax.dynamic_slice_in_dim(suscept, offset, owned, 0)
     updated = own_suscept[None, :] * (inducing[:, None] + demag)
-    block_mag = lax.all_gather(updated, "stn", axis=1, tiled=True)
+    ring = [updated]
+    for hop in range(3):
+        ring.append(lax.ppermute(ring[-1], "stn", [(dev, (dev + 1) % 4) for dev in range(4)]))
+    block_mag = jnp.roll(
+        jnp.concatenate(ring[::-1], axis=1), (lax.axis_index("stn") + 1) * ring[0].shape[1], axis=1
+    )
     moved = jnp.concatenate([cell_points, block_mag, size_h[None, :]], 0)
     field = source_field(stations, moved)
     predictions = lax.psum_scatter(

time: 83.3 us -> 86.2 us (1.035)
  waiting for transfers between devices: 0 us -> 7.79 us
  blocking collectives: 59.1 us -> 54 us
    ppermute x0 -> x3, waiting for transfers between devices: none -> 7.79 us  [shards(): lax.ppermute(ring[-1], 'stn', [(dev, (dev + 1) % 4) for dev in range(4)])]
    all_gather x1 -> x0, blocking collectives: 5.17 us -> none  [shards(): block_mag = lax.all_gather(updated, 'stn', axis=1, tiled=True)]
  transfers between devices with their start and end apart: 0 -> 3, of which waited for: 0 -> 3; matrix products, arithmetic and copies ran while one was open for 0% -> 1% of each run, Pallas kernels for 0% -> 0%
where the time goes in v1:
time: 86.2 us; the launch traced here: 85.7 us
  blocking collectives  54 us (63%)
  other arithmetic  19.5 us (23%)
  waiting for transfers between devices  7.79 us (9%)
  local copies, waits for them, and re-layouts  3.04 us (4%)
  between operations  1.38 us (2%)
    all_gather x1, blocking collectives, shards(): lax.all_gather(packed, 'cell', axis=1, tiled=True)  32.5 us
    unnamed x1, blocking collectives  21.4 us
    reduce_sum x3, other arithmetic, pair_field(): jnp.sum(weight * (projection * delta_x - source_piece[3][None, :]), axis=1)  17.7 us
    ppermute x3, waiting for transfers between devices, shards(): lax.ppermute(ring[-1], 'stn', [(dev, (dev + 1) % 4) for dev in range(4)])  7.79 us
  transfers between devices with their start and end apart: 3, of which 3 were waited for; matrix products, arithmetic and copies ran while one was open for 1% of the time, Pallas kernels for 0%

profile of v1, /device:TPU:0, one launch (start us, length us, event | category | flops | bytes accessed | tf_op | source)
XLA Modules:
  0.0 85.7 jit_solution(4546358705420506428)
XLA Ops:
  0.6 0.7 multiply_multiply_fusion.3
  1.3 0.7 constant_dynamic-slice_fusion.8
  2.0 0.8 pad_maximum_fusion
  2.8 32.5 %all_gather.3 = f32[7,8192]{1,0:T(8,128)S(1)} all-gather(f32[7,1024]{1,0:T(8,128)S(1)} %pad_maximum_fusion), channel_id=1, replica_groups=mesh['cell'=8,'stn'=4] {'cell'}, dimensions={1}, use_global_device_ids=true | all-gather | bytes 258048 | tf_op jit(solution)/shard_map/all_gather | solution.py:62
  35.3 0.0 copy-start
  35.3 0.0 copy-start.1
  35.3 11.8 %while.3 = (s32[]{:T(128)}, f32[3,256]{1,0:T(4,128)S(1)}, f32[2,7,4096]{2,1,0:T(8,128)S(1)}, f32[3,256]{1,0:T(4,128)S(1)}, s32[]{:T(128)}, /*index=5*/s32[]{:T(128)}, s32[]{}, s32[]{}, s32[]{}, s32[]{}, /*index=10*/s32[]{}, s32[]{}) while((s32[]{:T(128)}, f32[3,256]{1,0:T(4,128)S(1)}, f32[2,7,4096]{2,1,0:T(8,128)S(1)}, ...), condition=%wide.region_4.5_spmd.clone, body=%wide.region_0.4_spmd.clone.sunk | while | flops 32524552 | bytes 431331 | solution.py:48
  35.3 0.1 constant_dynamic-slice_fusion.10
  35.5 5.7 %fusion.44 = (f32[256]{0:T(256)S(1)}, f32[256]{0:T(256)S(1)}, f32[256]{0:T(256)S(1)}) fusion(f32[4096]{0:T(1024)S(1)} %bitcast.60, f32[4096]{0:T(1024)S(1)} %bitcast.62, f32[256]{0:T(256)S(1)} %bitcast.69, f32[4096]{0:T(1024)S(1)} %get-tuple-element.134, f32[4096]{0:T(1024)S(1)} %bitcast.63, f32[4096]{0:T(1024)S(1)} %bitcast.61, f32[256]{0:T(256)S(1)} %bitcast.68, ...), kind=kLoop, calls=%fused_computation.19.clone.1 | loop fusion | flops 32505088 | bytes 137216 | tf_op jit(solution)/shard_map/while/body/eval_jaxpr/reduce_sum | solution.py:34
  41.3 0.1 constant_dynamic-slice_fusion.10
  41.4 5.7 %fusion.44 = (f32[256]{0:T(256)S(1)}, f32[256]{0:T(256)S(1)}, f32[256]{0:T(256)S(1)}) fusion(f32[4096]{0:T(1024)S(1)} %bitcast.60, f32[4096]{0:T(1024)S(1)} %bitcast.62, f32[256]{0:T(256)S(1)} %bitcast.69, f32[4096]{0:T(1024)S(1)} %get-tuple-element.134, f32[4096]{0:T(1024)S(1)} %bitcast.63, f32[4096]{0:T(1024)S(1)} %bitcast.61, f32[256]{0:T(256)S(1)} %bitcast.68, ...), kind=kLoop, calls=%fused_computation.19.clone.1 | loop fusion | flops 32505088 | bytes 137216 | tf_op jit(solution)/shard_map/while/body/eval_jaxpr/reduce_sum | solution.py:34
  47.2 0.8 dynamic_slice.17
  47.9 0.0 copy-done.2
  47.9 0.1 add_multiply_fusion
  48.0 0.0 collective-permute-start
  48.0 3.0 %collective-permute-done = f32[3,256]{1,0:T(4,128)S(1)} collective-permute-done((f32[3,256]{1,0:T(4,128)S(1)}, f32[3,256]{1,0:T(4,128)S(1)}, u32[]{:S(2)}, u32[]{:S(2)}) %collective-permute-start) | collective-permute-done | bytes 3104 | tf_op jit(solution)/shard_map/ppermute | solution.py:67
  51.1 0.0 collective-permute-start.1
  51.1 0.0 copy-done
  51.1 3.0 %collective-permute-done.1 = f32[3,256]{1,0:T(4,128)S(1)} collective-permute-done((f32[3,256]{1,0:T(4,128)S(1)}, f32[3,256]{1,0:T(4,128)S(1)}, u32[]{:S(2)}, u32[]{:S(2)}) %collective-permute-start.1) | collective-permute-done | bytes 3104 | tf_op jit(solution)/shard_map/ppermute | solution.py:67
  54.1 0.0 collective-permute-start.2
  54.1 0.0 copy-done.1
  54.1 0.0 copy-done.4
  54.1 0.6 dynamic-slice.1
  55.4 1.7 %collective-permute-done.2 = f32[3,256]{1,0:T(4,128)S(1)} collective-permute-done((f32[3,256]{1,0:T(4,128)S(1)}, f32[3,256]{1,0:T(4,128)S(1)}, u32[]{:S(2)}, u32[]{:S(2)}) %collective-permute-start.2) | collective-permute-done | bytes 3104 | tf_op jit(solution)/shard_map/ppermute | solution.py:67
  57.1 0.1 constant_dynamic-update-slice_fusion.4
  57.2 0.1 constant_dynamic-update-slice_fusion
  57.3 0.1 fusion.38
  57.4 6.2 %fusion.27 = (f32[1024]{0:T(1024)S(1)}, f32[1024]{0:T(1024)S(1)}, f32[1024]{0:T(1024)S(1)}) fusion(f32[1024]{0:T(1024)S(1)} %bitcast.72, f32[1024]{0:T(1024)S(1)} %bitcast.75, f32[1024]{0:T(1024)S(1)} %bitcast.78, f32[1024]{0:T(1024)S(1)} %get-tuple-element.88, f32[1024]{0:T(1024)S(1)} %bitcast.73, f32[1024]{0:T(1024)S(1)} %bitcast.76, ...), kind=kLoop, calls=%fused_computation.55 | loop fusion | flops 32502784 | bytes 57344 | tf_op jit(solution)/shard_map/while/body/eval_jaxpr/reduce_sum | solution.py:34
  63.6 0.0 copy-done.3
  63.6 0.1 fusion.34
  63.7 21.4 %all-reduce = f32[1024]{0:T(1024)S(1)} all-reduce(f32[1024]{0:T(1024)S(1)} %fusion.34), channel_id=2, replica_groups=mesh['cell'=8,'stn'=4] {'cell'}, use_global_device_ids=true, to_apply=%region_9.10.clone | all-reduce | flops 1024 | bytes 8192
  85.1 0.6 dynamic-slice.2
  (18 shorter events, 0.1 us)
Async XLA Ops:
  35.3 12.6 %copy-start.2 = (f32[3]{0:T(128)S(1)}, f32[3]{0:T(128)}, u32[]{:S(2)}) copy-start(f32[3]{0:T(128)} %param.12) | copy-start | bytes 40
  35.3 15.7 %copy-start = (f32[3,1024]{1,0:T(4,128)S(1)}, f32[3,1024]{1,0:T(4,128)}, u32[]{:S(2)}) copy-start(f32[3,1024]{1,0:T(4,128)} %param.8) | copy-start | bytes 36868
  35.3 18.8 %copy-start.1 = (f32[3,1024]{1,0:T(4,128)S(1)}, f32[3,1024]{1,0:T(4,128)}, u32[]{:S(2)}) copy-start(f32[3,1024]{1,0:T(4,128)} %param.13) | copy-start | bytes 36868
  35.3 18.8 %copy-start.4 = (u32[32]{0:T(128)S(1)}, u32[32]{0:T(128)}, u32[]{:S(2)}) copy-start(u32[32]{0:T(128)} %constant.70) | copy-start | bytes 388
  48.0 15.6 %copy-start.3 = (f32[3,256]{1,0:T(4,128)}, f32[3,256]{1,0:T(4,128)S(1)}, u32[]{:S(2)}) copy-start(f32[3,256]{1,0:T(4,128)S(1)} %add_multiply_fusion) | copy-start | bytes 9220
  48.0 3.0 %collective-permute-start = (f32[3,256]{1,0:T(4,128)S(1)}, f32[3,256]{1,0:T(4,128)S(1)}, u32[]{:S(2)}, u32[]{:S(2)}) collective-permute-start(f32[3,256]{1,0:T(4,128)S(1)} %add_multiply_fusion), channel_id=1, source_target_pairs={{0,1},{1,2},{2,3},{3,0},{4,5},{5,6},{6,7},{7,4},{8,9},{9,10},{10,1... | collective-permute-start | bytes 9224 | tf_op jit(solution)/shard_map/ppermute | solution.py:67
  51.1 3.0 %collective-permute-start.1 = (f32[3,256]{1,0:T(4,128)S(1)}, f32[3,256]{1,0:T(4,128)S(1)}, u32[]{:S(2)}, u32[]{:S(2)}) collective-permute-start(f32[3,256]{1,0:T(4,128)S(1)} %collective-permute-done), channel_id=1, source_target_pairs={{0,1},{1,2},{2,3},{3,0},{4,5},{5,6},{6,7},{7,4},{8,9},{9,10},{10,1... | collective-permute-start | bytes 9224 | tf_op jit(solution)/shard_map/ppermute | solution.py:67
  54.1 3.0 %collective-permute-start.2 = (f32[3,256]{1,0:T(4,128)S(1)}, f32[3,256]{1,0:T(4,128)S(1)}, u32[]{:S(2)}, u32[]{:S(2)}) collective-permute-start(f32[3,256]{1,0:T(4,128)S(1)} %collective-permute-done.1), channel_id=1, source_target_pairs={{0,1},{1,2},{2,3},{3,0},{4,5},{5,6},{6,7},{7,4},{8,9},{9,10},{10,1... | collective-permute-start | bytes 9224 | tf_op jit(solution)/shard_map/ppermute | solution.py:67
